TPU v7x, 256 devices: a whole 4x4x8 slice. The times are simulated.
256 devices in a mesh: section: 8 (over x, y_lo), expert: 32 (over z, y_hi, core).
Axes of the slice: x: 4, y: 4 (y_hi: 2, y_lo: 2; y = y_hi * 2 + y_lo), z: 8, core: 2. Of those that a mesh axis runs over, the one named last changes fastest.
Arguments:
- fwd_inputs: bfloat16 [8, 4096, 7168], P('section', 'expert'), may hold values from -6 to 6
- fwd_gates: float32 [8, 4096, 8], P('section', 'expert'), may hold values from 0.1 to 1
- fwd_routes: int32 [8, 4096, 8], P('section', 'expert'), may hold values from 0 to 255, as said below
- bwd_saved: bfloat16 [8, 512, 7168], P('section', 'expert'), may hold values from -6 to 6
- bwd_cotangents: bfloat16 [8, 4096, 7168], P('section', 'expert'), may hold values from -0.59765625 to 0.59765625
- bwd_gates: float32 [8, 4096, 8], P('section', 'expert'), may hold values from 0.1 to 1
- bwd_routes: int32 [8, 4096, 8], P('section', 'expert'), may hold values from 0 to 255, as said below
- w_gate: bfloat16 [8, 7168, 4096], P('section', None, 'expert'), may hold values from -0.0625 to 0.0625
- w_up: bfloat16 [8, 7168, 4096], P('section', None, 'expert'), may hold values from -0.0625 to 0.0625
- w_down: bfloat16 [8, 4096, 7168], P('section', 'expert'), may hold values from -0.125 to 0.125
Outputs:
- fwd_outputs: bfloat16 [8, 4096, 7168], P('section', 'expert')
- bwd_input_grads: bfloat16 [8, 4096, 7168], P('section', 'expert')
- bwd_gate_grads: float32 [8, 4096, 8], P('section', 'expert')
Inputs may be any that keep to these rules, and one draw needn't show every extreme that they name: `fwd_routes`: each row names 8 different experts. In each aligned block of 128 rows of a section, each expert below 2 is named by at least half of 8 and at most 8 rows; for each such expert there is a section where every block has exactly 8. `bwd_routes`: as for fwd_routes.
All inputs are finite; a program needn't handle non-finite values.
Results may differ from a plain program's by a relative error of at most 0.008.
Values may be sent and summed in bfloat16 or wider, within the bound.
A program may use at most 128 MiB of HBM per device.

v0:
```python
import jax
import jax.numpy as jnp
from jax import lax
from jax.sharding import PartitionSpec as P

FLIGHT = 2
CAP = 8


def shifted(block, axis, distance):
    devices = range(lax.axis_size(axis))
    route = [((i - distance) % len(devices), i) for i in devices]
    return lax.ppermute(block, axis, route)


def tables(routes, gates):
    expert_ids = jnp.arange(FLIGHT, dtype=jnp.int32)
    route_hits = routes[:, None, :] == expert_ids[None, :, None]
    member = jnp.sum(route_hits.astype(jnp.int32), axis=2)
    position = jnp.cumsum(member, axis=0) - 1
    slot_ids = jnp.arange(CAP, dtype=jnp.int32)
    onehot = (member[None, :, :] == 1) & (position[None, :, :] == slot_ids[:, None, None])
    onehot = jnp.transpose(onehot, (2, 0, 1)).astype(jnp.float32)
    weight = jnp.sum(
        jnp.where(route_hits, gates[:, None, :], jnp.zeros_like(gates)[:, None, :]), axis=2
    )
    return (onehot, route_hits, weight)


def pack_slots(onehot, tokens):
    packed = jnp.einsum(
        "jct,td->jcd", onehot.astype(jnp.bfloat16), tokens, preferred_element_type=jnp.float32
    )
    return packed.astype(jnp.bfloat16)


def combine(onehot, weight, slot_values):
    return jnp.einsum(
        "jct,tj,jcd->td", onehot, weight, slot_values, precision=lax.Precision.HIGHEST
    )


def forward_rows(row_block, gate_cols, up_cols, down_rows):
    gate_pre = jnp.dot(row_block, gate_cols, preferred_element_type=jnp.float32)
    up_pre = jnp.dot(row_block, up_cols, preferred_element_type=jnp.float32)
    hidden = (jax.nn.silu(gate_pre) * up_pre).astype(jnp.bfloat16)
    return jnp.dot(hidden, down_rows, preferred_element_type=jnp.float32)


def backward_rows(row_block, cot_block, gate_cols, up_cols, down_rows):
    gate_pre = jnp.dot(row_block, gate_cols, preferred_element_type=jnp.float32)
    up_pre = jnp.dot(row_block, up_cols, preferred_element_type=jnp.float32)
    sigmoid = jax.nn.sigmoid(gate_pre)
    hidden = (jax.nn.silu(gate_pre) * up_pre).astype(jnp.bfloat16)
    contract = (((1,), (1,)), ((), ()))
    back_hidden = lax.dot_general(
        cot_block, down_rows, contract, preferred_element_type=jnp.float32
    )
    gate_term = jnp.sum(back_hidden * hidden.astype(jnp.float32), axis=1)
    grad_gate = (back_hidden * up_pre * sigmoid * (1.0 + gate_pre * (1.0 - sigmoid))).astype(
        jnp.bfloat16
    )
    grad_up = (back_hidden * jax.nn.silu(gate_pre)).astype(jnp.bfloat16)
    input_term = lax.dot_general(grad_gate, gate_cols, contract, preferred_element_type=jnp.float32)
    input_term = input_term + lax.dot_general(
        grad_up, up_cols, contract, preferred_element_type=jnp.float32
    )
    return (input_term, gate_term)


def body(
    fwd_inputs,
    fwd_gates,
    fwd_routes,
    bwd_saved,
    bwd_cotangents,
    bwd_gates,
    bwd_routes,
    w_gate,
    w_up,
    w_down,
):
    device_count = lax.axis_size("expert")
    group_size = device_count // FLIGHT
    model_width = fwd_inputs.shape[2]
    gate_cols = w_gate[0]
    up_cols = w_up[0]
    down_rows = w_down[0]
    arrived = shifted(fwd_inputs, "section", 1)[0]
    incoming = shifted(bwd_cotangents, "section", -1)[0]
    onehot_fwd, hits_fwd, weight_fwd = tables(fwd_routes[0], fwd_gates[0])
    packed_fwd = pack_slots(onehot_fwd, arrived)
    received = lax.all_to_all(
        jnp.repeat(packed_fwd, group_size, axis=0),
        "expert",
        split_axis=0,
        concat_axis=0,
        tiled=True,
    )
    partial_value = forward_rows(received.reshape(-1, model_width), gate_cols, up_cols, down_rows)
    partial_value = partial_value.astype(jnp.bfloat16).reshape(device_count, CAP, model_width)
    returned = lax.all_to_all(partial_value, "expert", split_axis=0, concat_axis=0, tiled=True)
    expert_out = jnp.sum(
        returned.reshape(FLIGHT, group_size, CAP, model_width).astype(jnp.float32), axis=1
    )
    fwd_outputs = combine(onehot_fwd, weight_fwd, expert_out).astype(jnp.bfloat16)
    onehot_bwd, hits_bwd, weight_bwd = tables(bwd_routes[0], bwd_gates[0])
    packed_x = bwd_saved[0].reshape(FLIGHT, CAP, model_width)
    packed_g = pack_slots(onehot_bwd, incoming)
    recv_x, recv_g = (
        lax.all_to_all(
            jnp.repeat(packed_x, group_size, axis=0),
            "expert",
            split_axis=0,
            concat_axis=0,
            tiled=True,
        ),
        lax.all_to_all(
            jnp.repeat(packed_g, group_size, axis=0),
            "expert",
            split_axis=0,
            concat_axis=0,
            tiled=True,
        ),
    )
    input_term, gate_term = backward_rows(
        recv_x.reshape(-1, model_width),
        recv_g.reshape(-1, model_width),
        gate_cols,
        up_cols,
        down_rows,
    )
    input_term = input_term.astype(jnp.bfloat16).reshape(device_count, CAP, model_width)
    gate_term = gate_term.astype(jnp.bfloat16).reshape(device_count, CAP)
    back_input, back_gate = (
        lax.all_to_all(input_term, "expert", split_axis=0, concat_axis=0, tiled=True),
        lax.all_to_all(gate_term, "expert", split_axis=0, concat_axis=0, tiled=True),
    )
    input_slot = jnp.sum(
        back_input.reshape(FLIGHT, group_size, CAP, model_width).astype(jnp.float32), axis=1
    )
    gate_slot = jnp.sum(back_gate.reshape(FLIGHT, group_size, CAP).astype(jnp.float32), axis=1)
    bwd_input_grads = combine(onehot_bwd, weight_bwd, input_slot).astype(jnp.bfloat16)
    slot_values = jnp.einsum("jct,jc->tj", onehot_bwd, gate_slot, precision=lax.Precision.HIGHEST)
    bwd_gate_grads = jnp.einsum(
        "tjk,tj->tk", hits_bwd.astype(jnp.float32), slot_values, precision=lax.Precision.HIGHEST
    )
    return (fwd_outputs[None], bwd_input_grads[None], bwd_gate_grads[None])


def solution(mesh):
    placed = (
        P("section", "expert", None),
        P("section", "expert", None),
        P("section", "expert", None),
        P("section", "expert", None),
        P("section", "expert", None),
        P("section", "expert", None),
        P("section", "expert", None),
        P("section", None, "expert"),
        P("section", None, "expert"),
        P("section", "expert", None),
    )
    return jax.shard_map(
        body,
        mesh=mesh,
        in_specs=placed,
        out_specs=(
            P("section", "expert", None),
            P("section", "expert", None),
            P("section", "expert", None),
        ),
        check_vma=False,
    )
```

profile of v0, /device:TPU:9, one launch (start us, length us, event | category | flops | bytes accessed | tf_op | source)
XLA Modules:
  0.0 502.8 jit_solution(1816363779351427582)
XLA Ops:
  0.6 3.3 broadcast_in_dim.62
  4.0 11.2 %all-to-all-start.3 = ((bf16[32,8,7168]{2,1,0:T(8,128)(2,1)}), bf16[32,8,7168]{2,1,0:T(8,128)(2,1)}, u32[]{:S(2)}, u32[]{:S(2)}) async-start(bf16[32,8,7168]{2,1,0:T(8,128)(2,1)} %bitcast.123), calls=%async_computation.3 | async-start | bytes 7340032 | tf_op jit(solution)/shard_map/all_to_all | solution.py:111
  16.7 77.4 %collective-permute-done.1 = bf16[1,128,7168]{2,1,0:T(8,128)(2,1)} collective-permute-done((bf16[1,128,7168]{2,1,0:T(8,128)(2,1)}, bf16[1,128,7168]{2,1,0:T(8,128)(2,1)}, u32[]{:S(2)}, u32[]{:S(2)}) %collective-permute-start.1) | collective-permute-done | bytes 1835040 | tf_op jit(solution)/shard_map/ppermute | solution.py:13
  95.9 4.6 all-to-all-done.3
  102.9 5.8 %all-to-all-start.2 = ((bf16[32,8,7168]{2,1,0:T(8,128)(2,1)}), bf16[32,8,7168]{2,1,0:T(8,128)(2,1)}, u32[]{:S(2)}, u32[]{:S(2)}) async-start(bf16[32,8,7168]{2,1,0:T(8,128)(2,1)} %bitcast.122), calls=%async_computation.2 | async-start | bytes 7340032 | tf_op jit(solution)/shard_map/all_to_all | solution.py:118
  108.7 6.1 %collective-permute-start = (bf16[1,128,7168]{2,1,0:T(8,128)(2,1)}, bf16[1,128,7168]{2,1,0:T(8,128)(2,1)}, u32[]{:S(2)}, u32[]{:S(2)}) collective-permute-start(bf16[1,128,7168]{2,1,0:T(8,128)(2,1)} %param.10), channel_id=1, source_target_pairs={{224,0},{0,32},{32,64},{64,96},{96,128},{128,160},{160,192},{192,2... | collective-permute-start | bytes 5505032 | tf_op jit(solution)/shard_map/ppermute | solution.py:13
  115.1 78.2 %collective-permute-done = bf16[1,128,7168]{2,1,0:T(8,128)(2,1)} collective-permute-done((bf16[1,128,7168]{2,1,0:T(8,128)(2,1)}, bf16[1,128,7168]{2,1,0:T(8,128)(2,1)}, u32[]{:S(2)}, u32[]{:S(2)}) %collective-permute-start) | collective-permute-done | bytes 1835040 | tf_op jit(solution)/shard_map/ppermute | solution.py:13
  198.6 15.4 %all-to-all-start = ((bf16[32,8,7168]{2,1,0:T(8,128)(2,1)}), bf16[32,8,7168]{2,1,0:T(8,128)(2,1)}, u32[]{:S(2)}, u32[]{:S(2)}) async-start(bf16[32,8,7168]{2,1,0:T(8,128)(2,1)} %bitcast.124), calls=%async_computation | async-start | bytes 7340032 | tf_op jit(solution)/shard_map/all_to_all | solution.py:93
  214.0 3.7 fusion.7
  217.8 3.3 fusion.9
  221.1 3.2 multiply_reduce_fusion
  225.0 5.6 %fusion.23 = f32[256,7168]{1,0:T(8,128)} fusion(bf16[1,7168,128]{2,1,0:T(8,128)(2,1)} %param.17, f32[256,128]{1,0:T(8,128)S(1)} %fusion.7, f32[256,128]{1,0:T(8,128)S(1)} %get-tuple-element.6, f32[256,128]{1,0:T(8,128)S(1)} %fusion.9), kind=kOutput, calls=%fused_computation.31 | convolution fusion | flops 470089728 | bytes 9568256 | tf_op jit(solution)/shard_map/dot_general | solution.py:64
  230.6 68.8 %all-to-all-done = bf16[32,8,7168]{2,1,0:T(8,128)(2,1)} async-done(((bf16[32,8,7168]{2,1,0:T(8,128)(2,1)}), bf16[32,8,7168]{2,1,0:T(8,128)(2,1)}, u32[]{:S(2)}, u32[]{:S(2)}) %all-to-all-start) | async-done | bytes 3670048 | tf_op jit(solution)/shard_map/all_to_all | solution.py:93
  299.4 4.8 all-to-all-start.5
  304.3 6.1 %fusion.1 = bf16[32,8,7168]{2,1,0:T(8,128)(2,1)} fusion(f32[256,7168]{1,0:T(8,128)} %fusion.23, bf16[1,7168,128]{2,1,0:T(8,128)(2,1)S(1)} %copy-done, f32[256,128]{1,0:T(8,128)S(1)} %get-tuple-element.6, f32[256,128]{1,0:T(8,128)S(1)} %fusion.7), kind=kOutput, calls=%fused_computation.3 | convolution fusion | flops 473628672 | bytes 13107200 | tf_op jit(solution)/shard_map/dot_general | solution.py:65
  310.4 3.2 all-to-all-done.5
  313.6 6.7 %all-to-all-start.4 = ((bf16[32,8,7168]{2,1,0:T(8,128)(2,1)}), bf16[32,8,7168]{2,1,0:T(8,128)(2,1)}, u32[]{:S(2)}, u32[]{:S(2)}) async-start(bf16[32,8,7168]{2,1,0:T(8,128)(2,1)} %fusion.1), calls=%async_computation.4 | async-start | bytes 7340032 | tf_op jit(solution)/shard_map/all_to_all | solution.py:136
  320.3 3.7 fusion.15
  324.0 6.6 %fusion.2 = bf16[32,8,7168]{2,1,0:T(8,128)(2,1)} fusion(bf16[1,128,7168]{2,1,0:T(8,128)(2,1)} %param.19, bf16[1,7168,128]{2,1,0:T(8,128)(2,1)S(1)} %copy-done, bf16[32,8,7168]{2,1,0:T(8,128)(2,1)} %all-to-all-done, f32[256,128]{1,0:T(8,128)S(1)} %fusion.15), kind=kOutput, calls=%fused_computation.4 | convolution fusion | flops 941555712 | bytes 11141120 | tf_op jit(solution)/shard_map/dot_general | solution.py:47
  330.6 75.1 %all-to-all-done.4 = bf16[32,8,7168]{2,1,0:T(8,128)(2,1)} async-done(((bf16[32,8,7168]{2,1,0:T(8,128)(2,1)}), bf16[32,8,7168]{2,1,0:T(8,128)(2,1)}, u32[]{:S(2)}, u32[]{:S(2)}) %all-to-all-start.4) | async-done | bytes 3670048 | tf_op jit(solution)/shard_map/all_to_all | solution.py:136
  405.6 4.9 all-to-all-start.1
  413.9 4.2 fusion.5
  418.1 77.8 %all-to-all-done.1 = bf16[32,8,7168]{2,1,0:T(8,128)(2,1)} async-done(((bf16[32,8,7168]{2,1,0:T(8,128)(2,1)}), bf16[32,8,7168]{2,1,0:T(8,128)(2,1)}, u32[]{:S(2)}, u32[]{:S(2)}) %all-to-all-start.1) | async-done | bytes 3670048 | tf_op jit(solution)/shard_map/all_to_all | solution.py:102
  498.5 4.2 fusion.6
  (38 shorter events, 18.0 us)
Async XLA Ops:
  0.6 217.1 %copy-start = (bf16[1,7168,128]{2,1,0:T(8,128)(2,1)S(1)}, bf16[1,7168,128]{2,1,0:T(8,128)(2,1)}, u32[]{:S(2)}) copy-start(bf16[1,7168,128]{2,1,0:T(8,128)(2,1)} %param.18) | copy-start | bytes 5505028
  4.0 12.4 %copy-start.2 = (s32[1,128,8]{1,2,0:T(8,128)S(1)}, s32[1,128,8]{1,2,0:T(8,128)}, u32[]{:S(2)}) copy-start(s32[1,128,8]{1,2,0:T(8,128)} %param.16) | copy-start | bytes 12292
  4.0 96.6 %all-to-all-start.3 = ((bf16[32,8,7168]{2,1,0:T(8,128)(2,1)}), bf16[32,8,7168]{2,1,0:T(8,128)(2,1)}, u32[]{:S(2)}, u32[]{:S(2)}) async-start(bf16[32,8,7168]{2,1,0:T(8,128)(2,1)} %bitcast.123), calls=%async_computation.3 | async-start | bytes 7340032 | tf_op jit(solution)/shard_map/all_to_all | solution.py:111
  15.2 78.9 %collective-permute-start.1 = (bf16[1,128,7168]{2,1,0:T(8,128)(2,1)}, bf16[1,128,7168]{2,1,0:T(8,128)(2,1)}, u32[]{:S(2)}, u32[]{:S(2)}) collective-permute-start(bf16[1,128,7168]{2,1,0:T(8,128)(2,1)} %param.14), channel_id=1, source_target_pairs={{32,0},{64,32},{96,64},{128,96},{160,128},{192,160},{224,192},{0,2... | collective-permute-start | bytes 5505032 | tf_op jit(solution)/shard_map/ppermute | solution.py:13
  102.9 11.9 %copy-start.3 = (s32[1,128,8]{1,2,0:T(8,128)S(1)}, s32[1,128,8]{1,2,0:T(8,128)}, u32[]{:S(2)}) copy-start(s32[1,128,8]{1,2,0:T(8,128)} %param.12) | copy-start | bytes 12292
  102.9 93.4 %all-to-all-start.2 = ((bf16[32,8,7168]{2,1,0:T(8,128)(2,1)}), bf16[32,8,7168]{2,1,0:T(8,128)(2,1)}, u32[]{:S(2)}, u32[]{:S(2)}) async-start(bf16[32,8,7168]{2,1,0:T(8,128)(2,1)} %bitcast.122), calls=%async_computation.2 | async-start | bytes 7340032 | tf_op jit(solution)/shard_map/all_to_all | solution.py:118
  108.7 84.7 %collective-permute-start = (bf16[1,128,7168]{2,1,0:T(8,128)(2,1)}, bf16[1,128,7168]{2,1,0:T(8,128)(2,1)}, u32[]{:S(2)}, u32[]{:S(2)}) collective-permute-start(bf16[1,128,7168]{2,1,0:T(8,128)(2,1)} %param.10), channel_id=1, source_target_pairs={{224,0},{0,32},{32,64},{64,96},{96,128},{128,160},{160,192},{192,2... | collective-permute-start | bytes 5505032 | tf_op jit(solution)/shard_map/ppermute | solution.py:13
  198.6 100.8 %all-to-all-start = ((bf16[32,8,7168]{2,1,0:T(8,128)(2,1)}), bf16[32,8,7168]{2,1,0:T(8,128)(2,1)}, u32[]{:S(2)}, u32[]{:S(2)}) async-start(bf16[32,8,7168]{2,1,0:T(8,128)(2,1)} %bitcast.124), calls=%async_computation | async-start | bytes 7340032 | tf_op jit(solution)/shard_map/all_to_all | solution.py:93
  217.8 3.3 copy-start.1
  299.4 14.1 %all-to-all-start.5 = ((bf16[32,1,8]{2,1,0:T(2,128)(2,1)}), bf16[32,1,8]{2,1,0:T(2,128)(2,1)S(1)}, u32[]{:S(2)}, u32[]{:S(2)}) async-start(bf16[32,1,8]{2,1,0:T(2,128)(2,1)} %convert_element_type.115), calls=%async_computation.5 | async-start | bytes 32768 | tf_op jit(solution)/shard_map/all_to_all | solution.py:137
  313.6 92.1 %all-to-all-start.4 = ((bf16[32,8,7168]{2,1,0:T(8,128)(2,1)}), bf16[32,8,7168]{2,1,0:T(8,128)(2,1)}, u32[]{:S(2)}, u32[]{:S(2)}) async-start(bf16[32,8,7168]{2,1,0:T(8,128)(2,1)} %fusion.1), calls=%async_computation.4 | async-start | bytes 7340032 | tf_op jit(solution)/shard_map/all_to_all | solution.py:136
  330.6 80.0 %copy-start.5 = (f32[1,128,8]{1,2,0:T(8,128)S(1)}, f32[1,128,8]{1,2,0:T(8,128)}, u32[]{:S(2)}) copy-start(f32[1,128,8]{1,2,0:T(8,128)} %param.11) | copy-start | bytes 12292
  330.6 80.2 %copy-start.4 = (f32[1,128,8]{1,2,0:T(8,128)S(1)}, f32[1,128,8]{1,2,0:T(8,128)}, u32[]{:S(2)}) copy-start(f32[1,128,8]{1,2,0:T(8,128)} %param.15) | copy-start | bytes 12292
  405.6 90.3 %all-to-all-start.1 = ((bf16[32,8,7168]{2,1,0:T(8,128)(2,1)}), bf16[32,8,7168]{2,1,0:T(8,128)(2,1)}, u32[]{:S(2)}, u32[]{:S(2)}) async-start(bf16[32,8,7168]{2,1,0:T(8,128)(2,1)} %fusion.2), calls=%async_computation.1 | async-start | bytes 7340032 | tf_op jit(solution)/shard_map/all_to_all | solution.py:102
where the time goes:
time: 504 us; the launch traced here: 503 us
  waiting for transfers between devices  386 us (77%)
  starting transfers between devices  56 us (11%)
  matrix products  44.5 us (9%)
  local copies, waits for them, and re-layouts  9.07 us (2%)
  other arithmetic  6.22 us (1%)
    ppermute x2, waiting for transfers between devices, shifted(): return lax.ppermute(block, axis, route)  156 us
    all_to_all x1, waiting for transfers between devices, body(): lax.all_to_all(partial_value, 'expert', split_axis=0, concat_axis=0, tile...  77.8 us
    all_to_all x1, waiting for transfers between devices, body(): lax.all_to_all(input_term, 'expert', split_axis=0, concat_axis=0, tiled=T...  75.1 us
    all_to_all x1, waiting for transfers between devices, body(): lax.all_to_all(jnp.repeat(packed_fwd, group_size, axis=0), 'expert', spli...  68.8 us
    all_to_all x1, starting transfers between devices, body(): lax.all_to_all(jnp.repeat(packed_fwd, group_size, axis=0), 'expert', spli...  15.4 us
    all_to_all x1, starting transfers between devices, body(): lax.all_to_all(jnp.repeat(packed_x, group_size, axis=0), 'expert', split_...  11.2 us
  transfers between devices with their start and end apart: 8, of which 8 were waited for; matrix products, arithmetic and copies ran while one was open for 9% of the time, Pallas kernels for 0%

commit v1 on v0

--- a/solution.py
+++ b/solution.py
@@ -86,10 +86,12 @@
     gate_cols = w_gate[0]
     up_cols = w_up[0]
     down_rows = w_down[0]
-    arrived = shifted(fwd_inputs, "section", 1)[0]
-    incoming = shifted(bwd_cotangents, "section", -1)[0]
     onehot_fwd, hits_fwd, weight_fwd = tables(fwd_routes[0], fwd_gates[0])
-    packed_fwd = pack_slots(onehot_fwd, arrived)
+    onehot_bwd, hits_bwd, weight_bwd = tables(bwd_routes[0], bwd_gates[0])
+    onehot_next = shifted(onehot_fwd.astype(jnp.bfloat16), "section", -1)
+    onehot_previous = shifted(onehot_bwd.astype(jnp.bfloat16), "section", 1)
+    packed_fwd = shifted(pack_slots(onehot_next, fwd_inputs[0]), "section", 1)
+    packed_g = shifted(pack_slots(onehot_previous, bwd_cotangents[0]), "section", -1)
     received = lax.all_to_all(
         jnp.repeat(packed_fwd, group_size, axis=0),
         "expert",
@@ -104,9 +106,7 @@
         returned.reshape(FLIGHT, group_size, CAP, model_width).astype(jnp.float32), axis=1
     )
     fwd_outputs = combine(onehot_fwd, weight_fwd, expert_out).astype(jnp.bfloat16)
-    onehot_bwd, hits_bwd, weight_bwd = tables(bwd_routes[0], bwd_gates[0])
     packed_x = bwd_saved[0].reshape(FLIGHT, CAP, model_width)
-    packed_g = pack_slots(onehot_bwd, incoming)
     recv_x, recv_g = (
         lax.all_to_all(
             jnp.repeat(packed_x, group_size, axis=0),

time: 504 us -> 494 us (0.980)
  starting transfers between devices: 56 us -> 48.3 us
    ppermute x2 -> x4, waiting for transfers between devices: 156 us -> 38.9 us  [shifted(): return lax.ppermute(block, axis, route)]
    all_to_all x1, waiting for transfers between devices: 4.65 us -> 61.3 us  [body(): lax.all_to_all(jnp.repeat(packed_x, group_size, axis=0), 'expert', split_...]
    all_to_all x1, waiting for transfers between devices: 1.07 us -> 57.5 us  [body(): lax.all_to_all(jnp.repeat(packed_g, group_size, axis=0), 'expert', split_...]
    all_to_all x1, starting transfers between devices: 15.4 us -> 6.6 us  [body(): lax.all_to_all(jnp.repeat(packed_fwd, group_size, axis=0), 'expert', spli...]
  transfers between devices with their start and end apart: 8 -> 10, of which waited for: 8 -> 10; matrix products, arithmetic and copies ran while one was open for 9% -> 9% of each run, Pallas kernels for 0% -> 0%
where the time goes in v1:
time: 494 us; the launch traced here: 492 us
  waiting for transfers between devices  384 us (78%)
  starting transfers between devices  48.3 us (10%)
  matrix products  43.2 us (9%)
  local copies, waits for them, and re-layouts  9.08 us (2%)
  other arithmetic  6.26 us (1%)
    all_to_all x1, waiting for transfers between devices, body(): lax.all_to_all(partial_value, 'expert', split_axis=0, concat_axis=0, tile...  77.8 us
    all_to_all x1, waiting for transfers between devices, body(): lax.all_to_all(input_term, 'expert', split_axis=0, concat_axis=0, tiled=T...  75.1 us
    all_to_all x1, waiting for transfers between devices, body(): lax.all_to_all(jnp.repeat(packed_fwd, group_size, axis=0), 'expert', spli...  70.7 us
    all_to_all x1, waiting for transfers between devices, body(): lax.all_to_all(jnp.repeat(packed_x, group_size, axis=0), 'expert', split_...  61.3 us
    all_to_all x1, waiting for transfers between devices, body(): lax.all_to_all(jnp.repeat(packed_g, group_size, axis=0), 'expert', split_...  57.5 us
    ppermute x4, waiting for transfers between devices, shifted(): return lax.ppermute(block, axis, route)  38.9 us
    all_to_all x1, starting transfers between devices, body(): lax.all_to_all(jnp.repeat(packed_x, group_size, axis=0), 'expert', split_...  11.2 us
  transfers between devices with their start and end apart: 10, of which 10 were waited for; matrix products, arithmetic and copies ran while one was open for 9% of the time, Pallas kernels for 0%

profile of v1, /device:TPU:9, one launch (start us, length us, event | category | flops | bytes accessed | tf_op | source)
XLA Modules:
  0.0 491.6 jit_solution(12061903805918102217)
XLA Ops:
  0.6 3.3 broadcast_in_dim.62
  4.0 11.2 %all-to-all-start.3 = ((bf16[32,8,7168]{2,1,0:T(8,128)(2,1)}), bf16[32,8,7168]{2,1,0:T(8,128)(2,1)}, u32[]{:S(2)}, u32[]{:S(2)}) async-start(bf16[32,8,7168]{2,1,0:T(8,128)(2,1)} %bitcast.121), calls=%async_computation.3 | async-start | bytes 7340032 | tf_op jit(solution)/shard_map/all_to_all | solution.py:111
  17.7 6.3 %collective-permute-done.2 = bf16[2,8,128]{2,1,0:T(8,128)(2,1)S(1)} collective-permute-done((bf16[2,8,128]{2,1,0:T(8,128)(2,1)S(1)}, bf16[2,8,128]{2,1,0:T(8,128)(2,1)S(1)}, u32[]{:S(2)}, u32[]{:S(2)}) %collective-permute-start.2) | collective-permute-done | bytes 4128 | tf_op jit(solution)/shard_map/ppermute | solution.py:13
  25.9 13.4 %collective-permute-done.3 = bf16[2,8,7168]{2,1,0:T(8,128)(2,1)S(1)} collective-permute-done((bf16[2,8,7168]{2,1,0:T(8,128)(2,1)S(1)}, bf16[2,8,7168]{2,1,0:T(8,128)(2,1)S(1)}, u32[]{:S(2)}, u32[]{:S(2)}) %collective-permute-start.3) | collective-permute-done | bytes 229408 | tf_op jit(solution)/shard_map/ppermute | solution.py:13
  39.3 61.3 %all-to-all-done.3 = bf16[32,8,7168]{2,1,0:T(8,128)(2,1)} async-done(((bf16[32,8,7168]{2,1,0:T(8,128)(2,1)}), bf16[32,8,7168]{2,1,0:T(8,128)(2,1)}, u32[]{:S(2)}, u32[]{:S(2)}) %all-to-all-start.3) | async-done | bytes 3670048 | tf_op jit(solution)/shard_map/all_to_all | solution.py:111
  102.9 5.1 %all-to-all-start.2 = ((bf16[32,8,7168]{2,1,0:T(8,128)(2,1)}), bf16[32,8,7168]{2,1,0:T(8,128)(2,1)}, u32[]{:S(2)}, u32[]{:S(2)}) async-start(bf16[32,8,7168]{2,1,0:T(8,128)(2,1)} %bitcast.120), calls=%async_computation.2 | async-start | bytes 7340032 | tf_op jit(solution)/shard_map/all_to_all | solution.py:118
  111.1 3.4 collective-permute-done
  116.3 3.5 collective-permute-start.1
  119.9 15.9 %collective-permute-done.1 = bf16[2,8,7168]{2,1,0:T(8,128)(2,1)S(1)} collective-permute-done((bf16[2,8,7168]{2,1,0:T(8,128)(2,1)S(1)}, bf16[2,8,7168]{2,1,0:T(8,128)(2,1)S(1)}, u32[]{:S(2)}, u32[]{:S(2)}) %collective-permute-start.1) | collective-permute-done | bytes 229408 | tf_op jit(solution)/shard_map/ppermute | solution.py:13
  135.8 57.5 %all-to-all-done.2 = bf16[32,8,7168]{2,1,0:T(8,128)(2,1)} async-done(((bf16[32,8,7168]{2,1,0:T(8,128)(2,1)}), bf16[32,8,7168]{2,1,0:T(8,128)(2,1)}, u32[]{:S(2)}, u32[]{:S(2)}) %all-to-all-start.2) | async-done | bytes 3670048 | tf_op jit(solution)/shard_map/all_to_all | solution.py:118
  195.6 6.6 %all-to-all-start = ((bf16[32,8,7168]{2,1,0:T(8,128)(2,1)}), bf16[32,8,7168]{2,1,0:T(8,128)(2,1)}, u32[]{:S(2)}, u32[]{:S(2)}) async-start(bf16[32,8,7168]{2,1,0:T(8,128)(2,1)} %bitcast.122), calls=%async_computation | async-start | bytes 7340032 | tf_op jit(solution)/shard_map/all_to_all | solution.py:95
  205.6 3.3 fusion.9
  212.9 4.1 fusion.23
  217.0 70.7 %all-to-all-done = bf16[32,8,7168]{2,1,0:T(8,128)(2,1)} async-done(((bf16[32,8,7168]{2,1,0:T(8,128)(2,1)}), bf16[32,8,7168]{2,1,0:T(8,128)(2,1)}, u32[]{:S(2)}, u32[]{:S(2)}) %all-to-all-start) | async-done | bytes 3670048 | tf_op jit(solution)/shard_map/all_to_all | solution.py:95
  287.7 4.8 all-to-all-start.5
  292.5 6.7 %fusion.1 = bf16[32,8,7168]{2,1,0:T(8,128)(2,1)} fusion(f32[256,7168]{1,0:T(8,128)} %fusion.23, bf16[1,7168,128]{2,1,0:T(8,128)(2,1)} %param.18, f32[256,128]{1,0:T(8,128)S(1)} %get-tuple-element.6, f32[256,128]{1,0:T(8,128)S(1)} %fusion.7), kind=kOutput, calls=%fused_computation.3 | convolution fusion | flops 473628672 | bytes 13107200 | tf_op jit(solution)/shard_map/dot_general | solution.py:65
  301.8 7.2 %all-to-all-start.4 = ((bf16[32,8,7168]{2,1,0:T(8,128)(2,1)}), bf16[32,8,7168]{2,1,0:T(8,128)(2,1)}, u32[]{:S(2)}, u32[]{:S(2)}) async-start(bf16[32,8,7168]{2,1,0:T(8,128)(2,1)} %fusion.1), calls=%async_computation.4 | async-start | bytes 7340032 | tf_op jit(solution)/shard_map/all_to_all | solution.py:136
  309.0 3.7 fusion.13
  312.7 6.6 %fusion.2 = bf16[32,8,7168]{2,1,0:T(8,128)(2,1)} fusion(bf16[1,128,7168]{2,1,0:T(8,128)(2,1)} %param.19, f32[256,128]{1,0:T(8,128)S(1)} %fusion.13, bf16[32,8,7168]{2,1,0:T(8,128)(2,1)} %all-to-all-done, bf16[1,7168,128]{2,1,0:T(8,128)(2,1)S(1)} %copy-done), kind=kOutput, calls=%fused_computation.4 | convolution fusion | flops 941555712 | bytes 11141120 | tf_op jit(solution)/shard_map/dot_general | solution.py:47
  319.4 75.1 %all-to-all-done.4 = bf16[32,8,7168]{2,1,0:T(8,128)(2,1)} async-done(((bf16[32,8,7168]{2,1,0:T(8,128)(2,1)}), bf16[32,8,7168]{2,1,0:T(8,128)(2,1)}, u32[]{:S(2)}, u32[]{:S(2)}) %all-to-all-start.4) | async-done | bytes 3670048 | tf_op jit(solution)/shard_map/all_to_all | solution.py:136
  394.4 4.9 all-to-all-start.1
  402.7 4.2 fusion.5
  406.9 77.8 %all-to-all-done.1 = bf16[32,8,7168]{2,1,0:T(8,128)(2,1)} async-done(((bf16[32,8,7168]{2,1,0:T(8,128)(2,1)}), bf16[32,8,7168]{2,1,0:T(8,128)(2,1)}, u32[]{:S(2)}, u32[]{:S(2)}) %all-to-all-start.1) | async-done | bytes 3670048 | tf_op jit(solution)/shard_map/all_to_all | solution.py:104
  487.3 4.2 fusion.6
  (46 shorter events, 29.9 us)
Async XLA Ops:
  0.6 201.6 %copy-start = (bf16[1,7168,128]{2,1,0:T(8,128)(2,1)S(1)}, bf16[1,7168,128]{2,1,0:T(8,128)(2,1)}, u32[]{:S(2)}) copy-start(bf16[1,7168,128]{2,1,0:T(8,128)(2,1)} %param.17) | copy-start | bytes 5505028
  4.0 11.2 %copy-start.3 = (s32[1,128,8]{1,2,0:T(8,128)S(1)}, s32[1,128,8]{1,2,0:T(8,128)}, u32[]{:S(2)}) copy-start(s32[1,128,8]{1,2,0:T(8,128)} %param.16) | copy-start | bytes 12292
  4.0 96.6 %all-to-all-start.3 = ((bf16[32,8,7168]{2,1,0:T(8,128)(2,1)}), bf16[32,8,7168]{2,1,0:T(8,128)(2,1)}, u32[]{:S(2)}, u32[]{:S(2)}) async-start(bf16[32,8,7168]{2,1,0:T(8,128)(2,1)} %bitcast.121), calls=%async_computation.3 | async-start | bytes 7340032 | tf_op jit(solution)/shard_map/all_to_all | solution.py:111
  15.6 8.3 %collective-permute-start.2 = (bf16[2,8,128]{2,1,0:T(8,128)(2,1)S(1)}, bf16[2,8,128]{2,1,0:T(8,128)(2,1)S(1)}, u32[]{:S(2)}, u32[]{:S(2)}) collective-permute-start(bf16[2,8,128]{2,1,0:T(8,128)(2,1)S(1)} %convert_convert_fusion), channel_id=1, source_target_pairs={{224,0},{0,32},{32,64},{64,96},{96,128},{128,160},{160,192},{192,2... | collective-permute-start | bytes 12296 | tf_op jit(solution)/shard_map/ppermute | solution.py:13
  25.8 13.5 %collective-permute-start.3 = (bf16[2,8,7168]{2,1,0:T(8,128)(2,1)S(1)}, bf16[2,8,7168]{2,1,0:T(8,128)(2,1)S(1)}, u32[]{:S(2)}, u32[]{:S(2)}) collective-permute-start(bf16[2,8,7168]{2,1,0:T(8,128)(2,1)S(1)} %convolution_convert_fusion.1), channel_id=1, source_target_pairs={{32,0},{64,32},{96,64},{128,96},{160,128},{192,160},{224,192},{0,2... | collective-permute-start | bytes 688136 | tf_op jit(solution)/shard_map/ppermute | solution.py:13
  102.9 5.1 %copy-start.4 = (s32[1,128,8]{1,2,0:T(8,128)S(1)}, s32[1,128,8]{1,2,0:T(8,128)}, u32[]{:S(2)}) copy-start(s32[1,128,8]{1,2,0:T(8,128)} %param.12) | copy-start | bytes 12292
  102.9 90.5 %all-to-all-start.2 = ((bf16[32,8,7168]{2,1,0:T(8,128)(2,1)}), bf16[32,8,7168]{2,1,0:T(8,128)(2,1)}, u32[]{:S(2)}, u32[]{:S(2)}) async-start(bf16[32,8,7168]{2,1,0:T(8,128)(2,1)} %bitcast.120), calls=%async_computation.2 | async-start | bytes 7340032 | tf_op jit(solution)/shard_map/all_to_all | solution.py:118
  108.3 6.2 %collective-permute-start = (bf16[2,8,128]{2,1,0:T(8,128)(2,1)S(1)}, bf16[2,8,128]{2,1,0:T(8,128)(2,1)S(1)}, u32[]{:S(2)}, u32[]{:S(2)}) collective-permute-start(bf16[2,8,128]{2,1,0:T(8,128)(2,1)S(1)} %convert_convert_fusion.1), channel_id=1, source_target_pairs={{32,0},{64,32},{96,64},{128,96},{160,128},{192,160},{224,192},{0,2... | collective-permute-start | bytes 12296 | tf_op jit(solution)/shard_map/ppermute | solution.py:13
  116.3 19.5 %collective-permute-start.1 = (bf16[2,8,7168]{2,1,0:T(8,128)(2,1)S(1)}, bf16[2,8,7168]{2,1,0:T(8,128)(2,1)S(1)}, u32[]{:S(2)}, u32[]{:S(2)}) collective-permute-start(bf16[2,8,7168]{2,1,0:T(8,128)(2,1)S(1)} %convolution_convert_fusion.2), channel_id=1, source_target_pairs={{224,0},{0,32},{32,64},{64,96},{96,128},{128,160},{160,192},{192,2... | collective-permute-start | bytes 688136 | tf_op jit(solution)/shard_map/ppermute | solution.py:13
  195.6 92.0 %all-to-all-start = ((bf16[32,8,7168]{2,1,0:T(8,128)(2,1)}), bf16[32,8,7168]{2,1,0:T(8,128)(2,1)}, u32[]{:S(2)}, u32[]{:S(2)}) async-start(bf16[32,8,7168]{2,1,0:T(8,128)(2,1)} %bitcast.122), calls=%async_computation | async-start | bytes 7340032 | tf_op jit(solution)/shard_map/all_to_all | solution.py:95
  202.3 3.3 copy-start.1
  205.6 3.3 copy-start.2
  287.7 14.1 %all-to-all-start.5 = ((bf16[32,1,8]{2,1,0:T(2,128)(2,1)}), bf16[32,1,8]{2,1,0:T(2,128)(2,1)S(1)}, u32[]{:S(2)}, u32[]{:S(2)}) async-start(bf16[32,1,8]{2,1,0:T(2,128)(2,1)} %convert_element_type.115), calls=%async_computation.5 | async-start | bytes 32768 | tf_op jit(solution)/shard_map/all_to_all | solution.py:137
  301.8 92.6 %all-to-all-start.4 = ((bf16[32,8,7168]{2,1,0:T(8,128)(2,1)}), bf16[32,8,7168]{2,1,0:T(8,128)(2,1)}, u32[]{:S(2)}, u32[]{:S(2)}) async-start(bf16[32,8,7168]{2,1,0:T(8,128)(2,1)} %fusion.1), calls=%async_computation.4 | async-start | bytes 7340032 | tf_op jit(solution)/shard_map/all_to_all | solution.py:136
  319.4 80.0 %copy-start.6 = (f32[1,128,8]{1,2,0:T(8,128)S(1)}, f32[1,128,8]{1,2,0:T(8,128)}, u32[]{:S(2)}) copy-start(f32[1,128,8]{1,2,0:T(8,128)} %param.11) | copy-start | bytes 12292
  319.4 80.2 %copy-start.5 = (f32[1,128,8]{1,2,0:T(8,128)S(1)}, f32[1,128,8]{1,2,0:T(8,128)}, u32[]{:S(2)}) copy-start(f32[1,128,8]{1,2,0:T(8,128)} %param.15) | copy-start | bytes 12292
  394.4 90.3 %all-to-all-start.1 = ((bf16[32,8,7168]{2,1,0:T(8,128)(2,1)}), bf16[32,8,7168]{2,1,0:T(8,128)(2,1)}, u32[]{:S(2)}, u32[]{:S(2)}) async-start(bf16[32,8,7168]{2,1,0:T(8,128)(2,1)} %fusion.2), calls=%async_computation.1 | async-start | bytes 7340032 | tf_op jit(solution)/shard_map/all_to_all | solution.py:104
